TPU v7x, 512 devices: a whole 4x4x16 slice. The times are simulated.
512 devices in a mesh: learn: 16 (over z), tp: 8 (over y_hi, x), rep: 4 (over y_lo, core).
Axes of the slice: x: 4, y: 4 (y_hi: 2, y_lo: 2; y = y_hi * 2 + y_lo), z: 16, core: 2. Of those that a mesh axis runs over, the one named last changes fastest.
Arguments:
- master: float32 [8192, 2048], P(('learn', 'rep'), 'tp'), may hold values from -0.0625 to 0.0625
- moment_one: float32 [8192, 2048], P(('learn', 'rep'), 'tp'), may hold values from -3 to 3
- moment_two: float32 [8192, 2048], P(('learn', 'rep'), 'tp'), may hold values from 0.25 to 4
- gradient: bfloat16 [8192, 2048], P(('learn', 'rep'), 'tp'), may hold values from -6 to 6
- hidden: bfloat16 [128, 4, 8192], P(('learn', 'rep'), None, 'tp'), may hold values from -12 to 12
- queries: bfloat16 [128, 4, 8192], P(('learn', 'rep'), None, 'tp'), may hold values from -135 to 135
- cache_keys: bfloat16 [128, 2048, 1024], P(('learn', 'rep'), None, 'tp'), may hold values from -4.5 to 4.5
- cache_values: bfloat16 [128, 2048, 1024], P(('learn', 'rep'), None, 'tp'), may hold values from -6 to 6
- lengths: int32 [128], P(('learn', 'rep')), may hold values from 512 to 2048
Outputs:
- new_master: float32 [8192, 2048], P(('learn', 'rep'), 'tp')
- new_moment_one: float32 [8192, 2048], P(('learn', 'rep'), 'tp')
- new_moment_two: float32 [8192, 2048], P(('learn', 'rep'), 'tp')
- fresh_kv: bfloat16 [128, 4, 2048], P(('learn', 'rep'), None, 'tp')
- attended: bfloat16 [128, 4, 8192], P(('learn', 'rep'), None, 'tp')
All inputs are finite; a program needn't handle non-finite values.
Results may differ from a plain program's by a relative error of at most 0.014.
Values may be sent and summed in bfloat16 or wider, within the bound.
No kernel may reach another device: no remote copies, remote signals or barrier semaphores. Data moves between devices by JAX's collectives and lax.ppermute only.
A program may use at most 64 MiB of HBM per device.

v0:
```python
import math

import jax
import jax.numpy as jnp
from jax import lax
from jax.sharding import PartitionSpec as P

H = 64
KVH = 8
HD = 128


beta_one = 0.9
beta_two = 0.999
learning_rate = 0.0001
weight_decay = 0.1
epsilon = 1e-08
correct_one = 0.9999734386011124
correct_two = 0.09520785288629038


def local(
    master, moment_one, moment_two, gradient, hidden, queries, cache_keys, cache_values, lengths
):
    grads = gradient.astype(jnp.float32)
    new_moment_one = beta_one * moment_one + (1.0 - beta_one) * grads
    new_moment_two = beta_two * moment_two + (1.0 - beta_two) * grads * grads
    update = new_moment_one / correct_one / (jnp.sqrt(new_moment_two / correct_two) + epsilon)
    new_master = master - learning_rate * (update + weight_decay * master)
    weights = new_master.astype(jnp.bfloat16)
    tokens = lax.all_gather(hidden, "tp", axis=2, tiled=True)
    row_count, step_count, width = tokens.shape
    flat_rows = tokens.reshape(row_count * step_count, width)
    columns = weights.shape[1]
    projected = jnp.dot(
        flat_rows,
        lax.all_gather(weights, ("learn", "rep"), axis=0, tiled=True),
        preferred_element_type=jnp.float32,
    )
    fresh_kv = projected.astype(jnp.bfloat16).reshape(row_count, step_count, columns)
    local_heads = columns // (2 * HD)
    group_size = H // KVH
    fresh_heads = fresh_kv.reshape(row_count, step_count, local_heads, 2, HD)
    new_keys = fresh_heads[:, :, :, 0, :]
    new_values = fresh_heads[:, :, :, 1, :]
    query_heads = queries.reshape(row_count, step_count, local_heads, group_size, HD)
    context = cache_keys.shape[1]
    key_cache = cache_keys.reshape(row_count, context, local_heads, HD)
    value_cache = cache_values.reshape(row_count, context, local_heads, HD)
    root_size = math.sqrt(HD)
    cache_scores = (
        jnp.einsum("bsgjd,bcgd->bsgjc", query_heads, key_cache, preferred_element_type=jnp.float32)
        / root_size
    )
    live_cache = jnp.arange(context)[None, :] < lengths[:, None]
    cache_scores = jnp.where(live_cache[:, None, None, None, :], cache_scores, jnp.float32(-1e30))
    new_scores = (
        jnp.einsum("bsgjd,btgd->bsgjt", query_heads, new_keys, preferred_element_type=jnp.float32)
        / root_size
    )
    causal = jnp.arange(step_count)[None, :] <= jnp.arange(step_count)[:, None]
    new_scores = jnp.where(causal[None, :, None, None, :], new_scores, jnp.float32(-1e30))
    peak = jnp.maximum(
        jnp.max(cache_scores, axis=-1, keepdims=True), jnp.max(new_scores, axis=-1, keepdims=True)
    )
    cache_expo = jnp.exp(cache_scores - peak)
    new_expo = jnp.exp(new_scores - peak)
    denominator = jnp.sum(cache_expo, axis=-1, keepdims=True) + jnp.sum(
        new_expo, axis=-1, keepdims=True
    )
    cache_probs = (cache_expo / denominator).astype(jnp.bfloat16)
    new_probs = (new_expo / denominator).astype(jnp.bfloat16)
    mixture = jnp.einsum(
        "bsgjc,bcgd->bsgjd", cache_probs, value_cache, preferred_element_type=jnp.float32
    )
    mixture = mixture + jnp.einsum(
        "bsgjt,btgd->bsgjd", new_probs, new_values, preferred_element_type=jnp.float32
    )
    attended = mixture.astype(jnp.bfloat16).reshape(
        row_count, step_count, local_heads * group_size * HD
    )
    return (new_master, new_moment_one, new_moment_two, fresh_kv, attended)


def solution(mesh):
    return jax.shard_map(
        local,
        mesh=mesh,
        in_specs=(
            P(("learn", "rep"), "tp"),
            P(("learn", "rep"), "tp"),
            P(("learn", "rep"), "tp"),
            P(("learn", "rep"), "tp"),
            P(("learn", "rep"), None, "tp"),
            P(("learn", "rep"), None, "tp"),
            P(("learn", "rep"), None, "tp"),
            P(("learn", "rep"), None, "tp"),
            P(("learn", "rep")),
        ),
        out_specs=(
            P(("learn", "rep"), "tp"),
            P(("learn", "rep"), "tp"),
            P(("learn", "rep"), "tp"),
            P(("learn", "rep"), None, "tp"),
            P(("learn", "rep"), None, "tp"),
        ),
        check_vma=False,
    )
```

profile of v0, /device:TPU:24, one launch (start us, length us, event | category | flops | bytes accessed | tf_op | source)
XLA Modules:
  0.0 150.5 jit_solution(10751678162535232198)
XLA Ops:
  7.2 0.0 copy-start
  7.2 0.0 copy-start.1
  7.2 0.0 all-gather.2.cloned.1.call-start
  7.2 2.0 %fusion.17 = (bf16[128,256]{1,0:T(8,128)(2,1)}, f32[128,256]{1,0:T(8,128)}, f32[128,256]{1,0:T(8,128)}, f32[128,256]{1,0:T(8,128)}) fusion(f32[128,256]{1,0:T(8,128)} %param.9, bf16[128,256]{1,0:T(8,128)(2,1)} %param.12, f32[128,256]{1,0:T(8,128)} %param.10, f32[128,256]{1,0:T(8,128)} %param.11), kind=kLoop, calls=%fused_computation.33 | loop fusion | flops 557056 | bytes 917504 | tf_op jit(solution)/shard_map/convert_element_type | solution.py:30
  9.3 0.0 all-gather.2.cloned.1.call-update
  9.3 0.7 reshape.125
  10.0 34.5 %all_gather.7 = bf16[2,4,8192]{2,1,0:T(4,128)(2,1)S(1)} all-gather(bf16[2,4,1024]{2,1,0:T(4,128)(2,1)} %param.13), channel_id=1, replica_groups=mesh['learn'=16,'tp'=8,'rep'=4] {'tp'}, dimensions={2}, use_global_device_ids=true | all-gather | bytes 147456 | tf_op jit(solution)/shard_map/all_gather | solution.py:31
  44.6 0.7 iota_compare_fusion
  45.3 0.0 copy-done
  45.3 0.5 fusion.20
  45.9 92.7 %all-gather.2.cloned.1.call-done = bf16[8192,256]{1,0:T(8,128)(2,1)} async-done(((bf16[128,256]{1,0:T(8,128)(2,1)}), bf16[8192,256]{1,0:T(8,128)(2,1)}) %all-gather.2.cloned.1.call-update) | async-done | bytes 4194320 | tf_op jit(solution)/shard_map/all_gather | solution.py:37
  138.6 2.8 %convolution_convert_fusion = bf16[256,8]{0,1:T(8,128)(2,1)S(1)} fusion(bf16[8192,256]{1,0:T(8,128)(2,1)} %all-gather.2.cloned.1.call-done, bf16[8,8192]{1,0:T(8,128)(2,1)S(1)} %reshape.123), kind=kOutput, calls=%fused_computation.10 | convolution fusion | flops 33556480 | bytes 4329472 | tf_op jit(solution)/shard_map/dot_general | solution.py:35
  141.4 0.6 reshape.124
  142.0 0.2 fusion.21
  142.3 0.2 fusion.9
  142.5 0.0 copy-done.1
  142.5 0.3 convolution_bitcast_fusion
  142.9 0.2 fusion.4
  143.1 0.6 reshape.130
  (5 shorter events, 0.1 us)
Async XLA Ops:
  7.2 38.1 %copy-start = (bf16[2,2048,128]{2,1,0:T(8,128)(2,1)S(1)}, bf16[2,2048,128]{2,1,0:T(8,128)(2,1)}, u32[]{:S(2)}) copy-start(bf16[2,2048,128]{2,1,0:T(8,128)(2,1)} %param.15) | copy-start | bytes 3145732
  7.2 135.3 %copy-start.1 = (bf16[2,2048,128]{2,1,0:T(8,128)(2,1)S(1)}, bf16[2,2048,128]{2,1,0:T(8,128)(2,1)}, u32[]{:S(2)}) copy-start(bf16[2,2048,128]{2,1,0:T(8,128)(2,1)} %param.16) | copy-start | bytes 3145732
  7.2 131.4 %all-gather.2.cloned.1.call-start = ((), (), s32[]{:S(2)}) async-start(), calls=%async_computation | async-start | bytes 4259840 | tf_op jit(solution)/shard_map/all_gather | solution.py:37
Sparse Core Ops, SparseCore 0:
  10.2 128.3 all-gather.1
where the time goes:
time: 153 us; the launch traced here: 151 us
  waiting for transfers between devices  92.7 us (61%)
  blocking collectives  34.5 us (23%)
  between operations  14.1 us (9%)
  matrix products  4.11 us (3%)
  other arithmetic  3.05 us (2%)
  local copies, waits for them, and re-layouts  2.01 us (1%)
    all_gather x1, waiting for transfers between devices, local(): lax.all_gather(weights, ('learn', 'rep'), axis=0, tiled=True)  92.7 us
    all_gather x1, blocking collectives, local(): tokens = lax.all_gather(hidden, 'tp', axis=2, tiled=True)  34.5 us
  transfers between devices with their start and end apart: 1, of which 1 were waited for; matrix products, arithmetic and copies ran while one was open for 1% of the time, Pallas kernels for 0%

commit v1 on v0

v1 whole, which is shorter than its diff:
```python
import math

import jax
import jax.numpy as jnp
from jax import lax
from jax.experimental import pallas as pl
from jax.experimental.pallas import tpu as pltpu
from jax.sharding import Mesh, PartitionSpec as P

H = 64
KVH = 8
HD = 128
GROUP = H // KVH

beta_one = 0.9
beta_two = 0.999
learning_rate = 0.0001
weight_decay = 0.1
epsilon = 1e-08
correct_one = 0.9999734386011124
correct_two = 0.09520785288629038

AXES = ("zpair", "zlow", "yfar", "x", "ynear", "core")
SIZES = (8, 2, 2, 4, 2, 2)
LEARN = ("zpair", "zlow")
TP = ("yfar", "x")
REP = ("ynear", "core")
ROWS = LEARN + REP

OFFSET = {0: (1, 2), 1: (1, 1), 2: (0, 2), 3: (0, 1), 4: (0, 0), 5: (0, 3), 6: (1, 0), 7: (1, 3)}


def landing(pair, block):
    far, along = OFFSET[(pair - block) % 8]
    return ((block // 4) ^ far) * 4 + (block % 4 + along) % 4


HOPS = [
    ((pair * 2 + low) * 8 + block, (block * 2 + low) * 8 + landing(pair, block))
    for pair in range(8)
    for low in range(2)
    for block in range(8)
]
VMEM = pl.BlockSpec(memory_space=pltpu.VMEM)
SMEM = pl.BlockSpec(memory_space=pltpu.SMEM)
PARAMS = pltpu.CompilerParams(vmem_limit_bytes=32 * 1024 * 1024)


def slots_kernel(x_ref, out_ref):
    x = x_ref[...].astype(jnp.float32)
    rows = jnp.concatenate([x[0], x[1]], axis=0).astype(jnp.bfloat16)
    for low in range(2):
        part = rows[:, 512 * low : 512 * (low + 1)]
        for t in range(8):
            out_ref[low, t] = part


def project_kernel(y_ref, w_ref, out_ref):
    here = lax.axis_index("zpair")
    w = w_ref[...]
    for low in range(2):
        rows = y_ref[low].astype(jnp.float32).reshape(64, 512).astype(jnp.bfloat16)
        part = jnp.dot(rows, w, preferred_element_type=jnp.float32)
        for t in range(8):
            far = (here // 4) ^ (t // 4)
            along = (t % 4 - here % 4 + 4) % 4
            away = jnp.where(
                far == 0,
                jnp.where(along == 0, 4, jnp.where(along == 1, 3, jnp.where(along == 2, 2, 5))),
                jnp.where(along == 0, 6, jnp.where(along == 1, 1, jnp.where(along == 2, 0, 7))),
            )
            pair = (here + away) % 8
            out_ref[pair, low] = part[8 * t : 8 * t + 8]


def cache_kernel(lengths_ref, q_ref, k_ref, v_ref, heads_ref, acc_ref, peak_ref, total_ref):
    q = q_ref[...].astype(jnp.float32)
    q = jnp.concatenate([q[0], q[1]], axis=0)
    heads = jnp.concatenate([q[:, HD * j : HD * (j + 1)] for j in range(GROUP)], axis=0)
    heads = heads.astype(jnp.bfloat16)
    heads_ref[...] = heads
    context = k_ref.shape[1]
    contract = (((1,), (1,)), ((), ()))
    scores = [
        lax.dot_general(heads, k_ref[b], contract, preferred_element_type=jnp.float32)
        for b in range(2)
    ]
    request = lax.broadcasted_iota(jnp.int32, (64, 1), 0) // 4 % 2
    limit = jnp.where(request == 0, lengths_ref[0], lengths_ref[1])
    slot = lax.broadcasted_iota(jnp.int32, (64, context), 1)
    score = jnp.where(request == 0, scores[0], scores[1]) * (1.0 / math.sqrt(HD))
    score = jnp.where(slot < limit, score, jnp.float32(-1e30))
    peak = jnp.max(score, axis=1, keepdims=True)
    expo = jnp.exp(score - peak)
    total = jnp.sum(expo, axis=1, keepdims=True)
    probs = expo.astype(jnp.bfloat16)
    mixed = [
        jnp.dot(probs, v_ref[b], preferred_element_type=jnp.float32) for b in range(2)
    ]
    acc_ref[...] = jnp.where(request == 0, mixed[0], mixed[1])
    peak_ref[...] = jnp.broadcast_to(peak, (64, HD))
    total_ref[...] = jnp.broadcast_to(total, (64, HD))


def finish_kernel(parts_ref, heads_ref, acc_ref, peak_ref, total_ref, fresh_ref, out_ref):
    fresh = jnp.sum(parts_ref[...], axis=0)
    fresh_ref[0] = fresh[:4].astype(jnp.bfloat16)
    fresh_ref[1] = fresh[4:].astype(jnp.bfloat16)
    fresh = fresh.astype(jnp.bfloat16)
    contract = (((1,), (1,)), ((), ()))
    score = lax.dot_general(
        heads_ref[...], fresh[:, :HD], contract, preferred_element_type=jnp.float32
    ) * (1.0 / math.sqrt(HD))
    row = lax.broadcasted_iota(jnp.int32, (64, 8), 0) % 8
    column = lax.broadcasted_iota(jnp.int32, (64, 8), 1)
    seen = (row // 4 == column // 4) & (column % 4 <= row % 4)
    score = jnp.where(seen, score, jnp.float32(-1e30))
    old_peak = peak_ref[...]
    peak = jnp.maximum(old_peak, jnp.max(score, axis=1, keepdims=True))
    keep = jnp.exp(old_peak - peak)
    expo = jnp.exp(score - peak[:, :8])
    total = total_ref[...] * keep + jnp.sum(expo, axis=1, keepdims=True)
    mixed = jnp.dot(expo.astype(jnp.bfloat16), fresh[:, HD:], preferred_element_type=jnp.float32)
    mixed = (acc_ref[...] * keep + mixed) / total
    for j in range(GROUP):
        block = mixed[8 * j : 8 * j + 8]
        out_ref[0, :, HD * j : HD * (j + 1)] = block[:4].astype(jnp.bfloat16)
        out_ref[1, :, HD * j : HD * (j + 1)] = block[4:].astype(jnp.bfloat16)


def shape(sizes, dtype):
    return jax.ShapeDtypeStruct(sizes, dtype)


def local(
    master, moment_one, moment_two, gradient, hidden, queries, cache_keys, cache_values, lengths
):
    f32, bf16 = jnp.float32, jnp.bfloat16
    moved = lax.ppermute(hidden, LEARN + TP, HOPS)

    grads = gradient.astype(f32)
    new_moment_one = beta_one * moment_one + (1.0 - beta_one) * grads
    new_moment_two = beta_two * moment_two + (1.0 - beta_two) * grads * grads
    update = new_moment_one / correct_one / (jnp.sqrt(new_moment_two / correct_two) + epsilon)
    new_master = master - learning_rate * (update + weight_decay * master)
    weights = lax.all_gather(new_master.astype(bf16), REP, axis=0, tiled=True)
    moved, weights = lax.optimization_barrier((moved, weights))

    slots = pl.pallas_call(
        slots_kernel,
        out_shape=shape((2, 8, 8, 512), bf16),
        in_specs=[VMEM],
        out_specs=VMEM,
        compiler_params=PARAMS,
        name="slots",
    )(moved)
    tokens = lax.all_to_all(slots.reshape(16, 8, 512), ("zlow",) + TP, 0, 0)
    parts = pl.pallas_call(
        project_kernel,
        out_shape=shape((8, 2, 8, 256), f32),
        in_specs=[VMEM, VMEM],
        out_specs=VMEM,
        compiler_params=PARAMS,
        name="project",
    )(tokens.reshape(2, 8, 8, 512), weights)
    parts, queries = lax.optimization_barrier((parts, queries))
    parts = lax.all_to_all(parts.reshape(16, 8, 256), LEARN, 0, 0)
    cached = pl.pallas_call(
        cache_kernel,
        out_shape=[shape((64, HD), bf16)] + [shape((64, HD), f32)] * 3,
        in_specs=[SMEM] + [VMEM] * 3,
        out_specs=[VMEM] * 4,
        compiler_params=PARAMS,
        cost_estimate=pl.CostEstimate(
            flops=4 * 64 * 4096 * 128, bytes_accessed=1 << 22, transcendentals=64 * 2048
        ),
        name="cache",
    )(lengths, queries, cache_keys, cache_values)
    fresh_kv, attended = pl.pallas_call(
        finish_kernel,
        out_shape=[shape((2, 4, 256), bf16), shape((2, 4, 1024), bf16)],
        in_specs=[VMEM] * 5,
        out_specs=[VMEM] * 2,
        compiler_params=PARAMS,
        name="finish",
    )(parts, *cached)
    return new_master, new_moment_one, new_moment_two, fresh_kv, attended


def solution(mesh):
    fine = Mesh(mesh.devices.reshape(SIZES), AXES)
    square = P(ROWS, TP)
    rows = P(ROWS, None, TP)
    return jax.shard_map(
        local,
        mesh=fine,
        in_specs=(square, square, square, square, rows, rows, rows, rows, P(ROWS)),
        out_specs=(square, square, square, rows, rows),
        check_vma=False,
    )
```

time: 153 us -> 62.2 us (0.41)
  the two profiles are of different devices: /device:TPU:24 before, /device:TPU:32 now
where the time goes in v1:
time: 62.2 us; the launch traced here: 61.9 us
  blocking collectives  26.2 us (42%)
  starting transfers between devices  17.3 us (28%)
  waiting for transfers between devices  12.5 us (20%)
  Pallas kernels  3.27 us (5%)
  other arithmetic  1.87 us (3%)
  between operations  0.7 us (1%)
    all_to_all x1, blocking collectives, local(): tokens = lax.all_to_all(slots.reshape(16, 8, 512), ('zlow',) + TP, 0, 0)  20.3 us
    all_to_all x1, waiting for transfers between devices, local(): parts = lax.all_to_all(parts.reshape(16, 8, 256), LEARN, 0, 0)  11.2 us
    all_to_all x1, starting transfers between devices, local(): parts = lax.all_to_all(parts.reshape(16, 8, 256), LEARN, 0, 0)  9.59 us
    ppermute x1, starting transfers between devices, local(): moved = lax.ppermute(hidden, LEARN + TP, HOPS)  7.69 us
    all_gather x1, blocking collectives, local(): weights = lax.all_gather(new_master.astype(bf16), REP, axis=0, tiled=True)  5.95 us
    convert_element_type x1, other arithmetic, local(): weights = lax.all_gather(new_master.astype(bf16), REP, axis=0, tiled=True)  1.87 us
    pallas_call x1, Pallas kernels, local(): pl.pallas_call(cache_kernel, out_shape=[shape((64, HD), bf16)] + [shape((...  1.44 us
    ppermute x1, waiting for transfers between devices, local(): moved = lax.ppermute(hidden, LEARN + TP, HOPS)  1.35 us
  transfers between devices with their start and end apart: 2, of which 2 were waited for; matrix products, arithmetic and copies ran while one was open for 3% of the time, Pallas kernels for 2%

profile of v1, /device:TPU:32, one launch (start us, length us, event | category | flops | bytes accessed | tf_op | source)
XLA Modules:
  0.0 61.9 jit_solution(14315934116430266096)
XLA Ops:
  0.6 0.0 copy-start.1
  0.6 0.0 copy-start
  0.7 7.7 %collective-permute-start = (bf16[2,4,1024]{2,1,0:T(4,128)(2,1)}, bf16[2,4,1024]{2,1,0:T(4,128)(2,1)S(1)}, u32[]{:S(2)}, u32[]{:S(2)}) collective-permute-start(bf16[2,4,1024]{2,1,0:T(4,128)(2,1)} %param.13), channel_id=1, source_target_pairs={{0,24},{4,80},{8,152},{12,200},{16,272},{20,344},{24,400},{28,448}... | collective-permute-start | bytes 49160 | tf_op jit(solution)/shard_map/ppermute | solution.py:139
  8.4 1.9 %fusion.2 = (bf16[128,256]{1,0:T(8,128)(2,1)S(1)}, f32[128,256]{1,0:T(8,128)}, f32[128,256]{1,0:T(8,128)}, f32[128,256]{1,0:T(8,128)}) fusion(f32[128,256]{1,0:T(8,128)} %param.9, bf16[128,256]{1,0:T(8,128)(2,1)} %param.12, f32[128,256]{1,0:T(8,128)} %param.10, f32[128,256]{1,0:T(8,128)} %param.11), kind=kLoop, calls=%fused_computation.5 | loop fusion | flops 557056 | bytes 917504 | tf_op jit(solution)/shard_map/convert_element_type | solution.py:146
  10.2 5.9 %all_gather.3.w_ref = bf16[512,256]{1,0:T(8,128)(2,1)S(1)} all-gather(bf16[128,256]{1,0:T(8,128)(2,1)S(1)} %get-tuple-element.25), channel_id=1, replica_groups=mesh['zpair'=8,'zlow'=2,'yfar'=2,'x'=4,'ynear'=2,'core'=2] {'ynear','core'}, dimensions={0}, use_global_device_ids=true | all-gather | bytes 327680 | tf_op jit(solution)/shard_map/all_gather | solution.py:146
  16.2 1.4 %collective-permute-done.x_ref = bf16[2,4,1024]{2,1,0:T(4,128)(2,1)S(1)} collective-permute-done((bf16[2,4,1024]{2,1,0:T(4,128)(2,1)}, bf16[2,4,1024]{2,1,0:T(4,128)(2,1)S(1)}, u32[]{:S(2)}, u32[]{:S(2)}) %collective-permute-start) | collective-permute-done | bytes 16416 | tf_op jit(solution)/shard_map/ppermute | solution.py:139
  17.5 20.3 %all_to_all.10 = bf16[16,8,512]{2,1,0:T(8,128)(2,1)S(1)} all-to-all(bf16[16,8,512]{2,1,0:T(8,128)(2,1)S(1)} %bitcast.3), channel_id=1, replica_groups=mesh['zpair'=8,'zlow'=2,'yfar'=2,'x'=4,'ynear'=2,'core'=2] {'zlow','yfar..., dimensions={0} | all-to-all | bytes 262144 | tf_op jit(solution)/shard_map/all_to_all | solution.py:157
  37.8 0.9 %project.1 = f32[8,2,8,256]{3,2,1,0:T(8,128)} custom-call(bf16[2,8,8,512]{3,2,1,0:T(8,128)(2,1)S(1)} %bitcast.4, bf16[512,256]{1,0:T(8,128)(2,1)S(1)} %all_gather.3.w_ref), custom_call_target="tpu_custom_call" | custom-call | tf_op jit(solution)/shard_map/project/pallas_call | solution.py:158
  38.7 0.0 copy-start.2
  38.7 0.0 copy-start.3
  38.7 9.6 %all-to-all-start.1 = ((f32[16,8,256]{2,1,0:T(8,128)}), f32[16,8,256]{2,1,0:T(8,128)S(1)}, u32[]{:S(2)}, u32[]{:S(2)}) async-start(f32[16,8,256]{2,1,0:T(8,128)} %bitcast.2), calls=%async_computation.1 | async-start | bytes 262144 | tf_op jit(solution)/shard_map/all_to_all | solution.py:167
  48.3 0.0 copy-done.1
  48.3 0.0 copy-done
  48.3 0.0 copy-done.2
  48.3 0.0 copy-done.3
  48.3 1.4 %cache.1 = (bf16[64,128]{1,0:T(8,128)(2,1)S(1)}, f32[64,128]{1,0:T(8,128)S(1)}, f32[64,128]{1,0:T(8,128)S(1)}, f32[64,128]{1,0:T(8,128)S(1)}) custom-call(s32[2]{0:T(128)S(1)} %copy-done.3, bf16[2,4,1024]{2,1,0:T(4,128)(2,1)S(1)} %copy-done.2, bf16[2,2048,128]{2,1,0:T(8,128)(2,1)S(1)} %copy-done, bf16[2,2048,128]{2,1,0:T(8,128)(2,1)S(1)} %copy-done.1), custom_call_target="tpu_custom_call" | custom-call | flops 134217728 | bytes 4194304 | tf_op jit(solution)/shard_map/cache/pallas_call | solution.py:168
  49.7 11.2 %all-to-all-done.1.parts_ref = f32[16,8,256]{2,1,0:T(8,128)S(1)} async-done(((f32[16,8,256]{2,1,0:T(8,128)}), f32[16,8,256]{2,1,0:T(8,128)S(1)}, u32[]{:S(2)}, u32[]{:S(2)}) %all-to-all-start.1) | async-done | bytes 131104 | tf_op jit(solution)/shard_map/all_to_all | solution.py:167
  60.9 1.0 %finish.1 = (bf16[2,4,256]{2,1,0:T(4,128)(2,1)}, bf16[2,4,1024]{2,1,0:T(4,128)(2,1)}) custom-call(f32[16,8,256]{2,1,0:T(8,128)S(1)} %all-to-all-done.1.parts_ref, bf16[64,128]{1,0:T(8,128)(2,1)S(1)} %get-tuple-element.19.heads_ref, f32[64,128]{1,0:T(8,128)S(1)} %get-tuple-element.20.acc_ref, f32[64,128]{1,0:T(8,128)S(1)} %get-tuple-element.21.peak_ref, ...), custom_call_target="tpu_custom_call" | custom-call | tf_op jit(solution)/shard_map/finish/pallas_call | solution.py:179
  (1 shorter events, 0.0 us)
Async XLA Ops:
  0.6 47.6 %copy-start.1 = (bf16[2,2048,128]{2,1,0:T(8,128)(2,1)S(1)}, bf16[2,2048,128]{2,1,0:T(8,128)(2,1)}, u32[]{:S(2)}) copy-start(bf16[2,2048,128]{2,1,0:T(8,128)(2,1)} %v_ref.1) | copy-start | bytes 3145732
  0.6 47.6 %copy-start = (bf16[2,2048,128]{2,1,0:T(8,128)(2,1)S(1)}, bf16[2,2048,128]{2,1,0:T(8,128)(2,1)}, u32[]{:S(2)}) copy-start(bf16[2,2048,128]{2,1,0:T(8,128)(2,1)} %k_ref.1) | copy-start | bytes 3145732
  0.7 16.9 %collective-permute-start = (bf16[2,4,1024]{2,1,0:T(4,128)(2,1)}, bf16[2,4,1024]{2,1,0:T(4,128)(2,1)S(1)}, u32[]{:S(2)}, u32[]{:S(2)}) collective-permute-start(bf16[2,4,1024]{2,1,0:T(4,128)(2,1)} %param.13), channel_id=1, source_target_pairs={{0,24},{4,80},{8,152},{12,200},{16,272},{20,344},{24,400},{28,448}... | collective-permute-start | bytes 49160 | tf_op jit(solution)/shard_map/ppermute | solution.py:139
  38.7 9.6 %copy-start.2 = (bf16[2,4,1024]{2,1,0:T(4,128)(2,1)S(1)}, bf16[2,4,1024]{2,1,0:T(4,128)(2,1)}, u32[]{:S(2)}) copy-start(bf16[2,4,1024]{2,1,0:T(4,128)(2,1)} %q_ref) | copy-start | bytes 49156
  38.7 9.6 %copy-start.3 = (s32[2]{0:T(128)S(1)}, s32[2]{0:T(128)}, u32[]{:S(2)}) copy-start(s32[2]{0:T(128)} %lengths_ref.1) | copy-start | bytes 28
  38.7 22.2 %all-to-all-start.1 = ((f32[16,8,256]{2,1,0:T(8,128)}), f32[16,8,256]{2,1,0:T(8,128)S(1)}, u32[]{:S(2)}, u32[]{:S(2)}) async-start(f32[16,8,256]{2,1,0:T(8,128)} %bitcast.2), calls=%async_computation.1 | async-start | bytes 262144 | tf_op jit(solution)/shard_map/all_to_all | solution.py:167

commit v2 on v1

--- a/solution.py
+++ b/solution.py
@@ -41,6 +41,8 @@
     for low in range(2)
     for block in range(8)
 ]
+BLOCKS = [(i + 4) % 8 for i in range(8)]
+PAIRS = [(i + 4) % 8 for i in range(8)]
 VMEM = pl.BlockSpec(memory_space=pltpu.VMEM)
 SMEM = pl.BlockSpec(memory_space=pltpu.SMEM)
 PARAMS = pltpu.CompilerParams(vmem_limit_bytes=32 * 1024 * 1024)
@@ -49,28 +51,28 @@
 def slots_kernel(x_ref, out_ref):
     x = x_ref[...].astype(jnp.float32)
     rows = jnp.concatenate([x[0], x[1]], axis=0).astype(jnp.bfloat16)
-    for low in range(2):
-        part = rows[:, 512 * low : 512 * (low + 1)]
-        for t in range(8):
-            out_ref[low, t] = part
-
-
-def project_kernel(y_ref, w_ref, out_ref):
+    for t in range(8):
+        out_ref[t] = rows
+
+
+def project_kernel(y_ref, own_ref, other_ref, out_ref):
     here = lax.axis_index("zpair")
-    w = w_ref[...]
-    for low in range(2):
-        rows = y_ref[low].astype(jnp.float32).reshape(64, 512).astype(jnp.bfloat16)
-        part = jnp.dot(rows, w, preferred_element_type=jnp.float32)
-        for t in range(8):
-            far = (here // 4) ^ (t // 4)
-            along = (t % 4 - here % 4 + 4) % 4
-            away = jnp.where(
-                far == 0,
-                jnp.where(along == 0, 4, jnp.where(along == 1, 3, jnp.where(along == 2, 2, 5))),
-                jnp.where(along == 0, 6, jnp.where(along == 1, 1, jnp.where(along == 2, 0, 7))),
-            )
-            pair = (here + away) % 8
-            out_ref[pair, low] = part[8 * t : 8 * t + 8]
+    low = lax.axis_index("zlow")
+    rows = y_ref[...].astype(jnp.float32).reshape(64, 1024)
+    first, second = rows[:, :512], rows[:, 512:]
+    mine = jnp.where(low == 0, first, second).astype(jnp.bfloat16)
+    theirs = jnp.where(low == 0, second, first).astype(jnp.bfloat16)
+    part = jnp.dot(mine, own_ref[...], preferred_element_type=jnp.float32)
+    part = part + jnp.dot(theirs, other_ref[...], preferred_element_type=jnp.float32)
+    for i, t in enumerate(BLOCKS):
+        far = (here // 4) ^ (t // 4)
+        along = (t % 4 - here % 4 + 4) % 4
+        away = jnp.where(
+            far == 0,
+            jnp.where(along == 0, 4, jnp.where(along == 1, 3, jnp.where(along == 2, 2, 5))),
+            jnp.where(along == 0, 6, jnp.where(along == 1, 1, jnp.where(along == 2, 0, 7))),
+        )
+        out_ref[(here + away + 8 - PAIRS[0]) % 8] = part[8 * i : 8 * i + 8]
 
 
 def cache_kernel(lengths_ref, q_ref, k_ref, v_ref, heads_ref, acc_ref, peak_ref, total_ref):
@@ -138,33 +140,40 @@
     f32, bf16 = jnp.float32, jnp.bfloat16
     moved = lax.ppermute(hidden, LEARN + TP, HOPS)
 
-    grads = gradient.astype(f32)
-    new_moment_one = beta_one * moment_one + (1.0 - beta_one) * grads
-    new_moment_two = beta_two * moment_two + (1.0 - beta_two) * grads * grads
-    update = new_moment_one / correct_one / (jnp.sqrt(new_moment_two / correct_two) + epsilon)
-    new_master = master - learning_rate * (update + weight_decay * master)
-    weights = lax.all_gather(new_master.astype(bf16), REP, axis=0, tiled=True)
+    def adamw(master, moment_one, moment_two, gradient):
+        grads = gradient.astype(f32)
+        new_moment_one = beta_one * moment_one + (1.0 - beta_one) * grads
+        new_moment_two = beta_two * moment_two + (1.0 - beta_two) * grads * grads
+        update = new_moment_one / correct_one / (jnp.sqrt(new_moment_two / correct_two) + epsilon)
+        new_master = master - learning_rate * (update + weight_decay * master)
+        return new_master, new_moment_one, new_moment_two
+
+    weights = adamw(master, moment_one, moment_two, gradient)[0].astype(bf16)
+    weights = lax.all_gather(weights, REP, axis=0, tiled=True)
     moved, weights = lax.optimization_barrier((moved, weights))
-
+    others = lax.ppermute(weights, "zlow", [(0, 1), (1, 0)])
     slots = pl.pallas_call(
         slots_kernel,
-        out_shape=shape((2, 8, 8, 512), bf16),
+        out_shape=shape((8, 8, 1024), bf16),
         in_specs=[VMEM],
         out_specs=VMEM,
         compiler_params=PARAMS,
         name="slots",
     )(moved)
-    tokens = lax.all_to_all(slots.reshape(16, 8, 512), ("zlow",) + TP, 0, 0)
+    tokens = lax.all_to_all(slots, TP, 0, 0, axis_index_groups=[BLOCKS])
     parts = pl.pallas_call(
         project_kernel,
-        out_shape=shape((8, 2, 8, 256), f32),
-        in_specs=[VMEM, VMEM],
+        out_shape=shape((8, 8, 256), f32),
+        in_specs=[VMEM] * 3,
         out_specs=VMEM,
         compiler_params=PARAMS,
         name="project",
-    )(tokens.reshape(2, 8, 8, 512), weights)
-    parts, queries = lax.optimization_barrier((parts, queries))
-    parts = lax.all_to_all(parts.reshape(16, 8, 256), LEARN, 0, 0)
+    )(tokens, weights, others)
+    parts, queries, *state = lax.optimization_barrier(
+        (parts, queries, master, moment_one, moment_two, gradient)
+    )
+    new_master, new_moment_one, new_moment_two = adamw(*state)
+    parts = lax.all_to_all(parts, "zpair", 0, 0, axis_index_groups=[PAIRS])
     cached = pl.pallas_call(
         cache_kernel,
         out_shape=[shape((64, HD), bf16)] + [shape((64, HD), f32)] * 3,

time: 62.2 us -> 55 us (0.88)
  the two profiles are of different devices: /device:TPU:32 before, /device:TPU:24 now
where the time goes in v2:
time: 55 us; the launch traced here: 54.6 us
  starting transfers between devices  31.1 us (57%)
  blocking collectives  16.5 us (30%)
  Pallas kernels  3.23 us (6%)
  other arithmetic  1.98 us (4%)
  local copies, waits for them, and re-layouts  0.74 us (1%)
  between operations  0.74 us (1%)
    ppermute x1, starting transfers between devices, local(): moved = lax.ppermute(hidden, LEARN + TP, HOPS)  15.9 us
    all_to_all x1, starting transfers between devices, local(): parts = lax.all_to_all(parts, 'zpair', 0, 0, axis_index_groups=[PAIRS])  12.3 us
    all_to_all x1, blocking collectives, local(): tokens = lax.all_to_all(slots, TP, 0, 0, axis_index_groups=[BLOCKS])  10.7 us
    all_gather x1, blocking collectives, local(): weights = lax.all_gather(weights, REP, axis=0, tiled=True)  5.79 us
    ppermute x1, starting transfers between devices, local(): others = lax.ppermute(weights, 'zlow', [(0, 1), (1, 0)])  2.92 us
    pallas_call x1, Pallas kernels, local(): pl.pallas_call(cache_kernel, out_shape=[shape((64, HD), bf16)] + [shape((...  1.44 us
    convert_element_type x1, other arithmetic, local(): weights = adamw(master, moment_one, moment_two, gradient)[0].astype(bf16)  1.18 us
  transfers between devices with their start and end apart: 3, of which 1 were waited for; matrix products, arithmetic and copies ran while one was open for 4% of the time, Pallas kernels for 3%

profile of v2, /device:TPU:24, one launch (start us, length us, event | category | flops | bytes accessed | tf_op | source)
XLA Modules:
  0.0 54.6 jit_solution(2002541546356861203)
XLA Ops:
  0.6 0.0 copy-start.1
  0.6 0.0 copy-start
  0.7 15.9 %collective-permute-start = (bf16[2,4,1024]{2,1,0:T(4,128)(2,1)}, bf16[2,4,1024]{2,1,0:T(4,128)(2,1)S(1)}, u32[]{:S(2)}, u32[]{:S(2)}) collective-permute-start(bf16[2,4,1024]{2,1,0:T(4,128)(2,1)} %param.13), channel_id=1, source_target_pairs={{0,24},{4,80},{8,152},{12,200},{16,272},{20,344},{24,400},{28,448}... | collective-permute-start | bytes 49160 | tf_op jit(solution)/shard_map/ppermute | solution.py:141
  16.5 1.2 %fusion.12 = bf16[128,256]{1,0:T(8,128)(2,1)S(1)} fusion(f32[128,256]{1,0:T(8,128)} %param.9, f32[128,256]{1,0:T(8,128)} %param.11, bf16[128,256]{1,0:T(8,128)(2,1)} %param.12, f32[128,256]{1,0:T(8,128)} %param.10), kind=kLoop, calls=%fused_computation.17 | loop fusion | flops 557056 | bytes 524288 | tf_op jit(solution)/shard_map/convert_element_type | solution.py:151
  17.7 5.8 %all_gather.3.own_ref = bf16[512,256]{1,0:T(8,128)(2,1)S(1)} all-gather(bf16[128,256]{1,0:T(8,128)(2,1)S(1)} %fusion.12), channel_id=1, replica_groups=mesh['zpair'=8,'zlow'=2,'yfar'=2,'x'=4,'ynear'=2,'core'=2] {'ynear','core'}, dimensions={0}, use_global_device_ids=true | all-gather | bytes 327680 | tf_op jit(solution)/shard_map/all_gather | solution.py:152
  23.5 0.0 collective-permute-done.x_ref
  23.5 2.9 %collective-permute-start.1 = (bf16[512,256]{1,0:T(8,128)(2,1)S(1)}, bf16[512,256]{1,0:T(8,128)(2,1)S(1)}, u32[]{:S(2)}, u32[]{:S(2)}) collective-permute-start(bf16[512,256]{1,0:T(8,128)(2,1)S(1)} %all_gather.3.own_ref), channel_id=1, source_target_pairs={{0,32},{32,0},{1,33},{33,1},{2,34},{34,2},{3,35},{35,3},{4,36},{36... | collective-permute-start | bytes 786440 | tf_op jit(solution)/shard_map/ppermute | solution.py:154
  26.4 10.7 %all_to_all.10.y_ref = bf16[8,8,1024]{2,1,0:T(8,128)(2,1)S(1)} all-to-all(bf16[8,8,1024]{2,1,0:T(8,128)(2,1)S(1)} %slots.1), channel_id=1, replica_groups={{16,20,24,28,0,4,8,12},{17,21,25,29,1,5,9,13},{18,22,26,30,2,6,10,14},{..., dimensions={0} | all-to-all | bytes 262144 | tf_op jit(solution)/shard_map/all_to_all | solution.py:163
  37.1 0.0 collective-permute-done.1.other_ref
  37.1 0.8 %project.1 = f32[8,8,256]{2,1,0:T(8,128)} custom-call(bf16[8,8,1024]{2,1,0:T(8,128)(2,1)S(1)} %all_to_all.10.y_ref, bf16[512,256]{1,0:T(8,128)(2,1)S(1)} %all_gather.3.own_ref, bf16[512,256]{1,0:T(8,128)(2,1)S(1)} %collective-permute-done.1.other_ref), custom_call_target="tpu_custom_call" | custom-call | tf_op jit(solution)/shard_map/project/pallas_call | solution.py:164
  38.0 0.0 copy-start.3
  38.0 12.3 %all-to-all-start.1 = ((f32[8,8,256]{2,1,0:T(8,128)}), f32[8,8,256]{2,1,0:T(8,128)S(1)}, u32[]{:S(2)}, u32[]{:S(2)}) async-start(f32[8,8,256]{2,1,0:T(8,128)} %project.1), calls=%async_computation.1 | async-start | bytes 131072 | tf_op jit(solution)/shard_map/all_to_all | solution.py:176
  50.3 0.0 copy-done.1
  50.3 0.0 copy-done
  50.3 0.0 copy-done.3
  50.3 0.0 copy-start.2
  50.3 0.7 %copy-done.2 = bf16[2,4,1024]{2,1,0:T(4,128)(2,1)S(1)} copy-done((bf16[2,4,1024]{2,1,0:T(4,128)(2,1)S(1)}, bf16[2,4,1024]{2,1,0:T(4,128)(2,1)}, u32[]{:S(2)}) %copy-start.2) | copy-done | bytes 16408
  51.0 0.0 copy-start.4
  51.0 0.0 copy-start.5
  51.0 0.0 copy-start.6
  51.0 0.0 copy-start.7
  51.0 1.4 %cache.1 = (bf16[64,128]{1,0:T(8,128)(2,1)S(1)}, f32[64,128]{1,0:T(8,128)S(1)}, f32[64,128]{1,0:T(8,128)S(1)}, f32[64,128]{1,0:T(8,128)S(1)}) custom-call(s32[2]{0:T(128)S(1)} %copy-done.3, bf16[2,4,1024]{2,1,0:T(4,128)(2,1)S(1)} %copy-done.2, bf16[2,2048,128]{2,1,0:T(8,128)(2,1)S(1)} %copy-done, bf16[2,2048,128]{2,1,0:T(8,128)(2,1)S(1)} %copy-done.1), custom_call_target="tpu_custom_call" | custom-call | flops 134217728 | bytes 4194304 | tf_op jit(solution)/shard_map/cache/pallas_call | solution.py:177
  52.5 0.0 copy-done.4
  52.5 0.0 copy-done.5
  52.5 0.0 copy-done.6
  52.5 0.0 copy-done.7
  52.5 0.8 %multiply_subtract_fusion = (f32[128,256]{1,0:T(8,128)}, f32[128,256]{1,0:T(8,128)}, f32[128,256]{1,0:T(8,128)}) fusion(f32[128,256]{1,0:T(8,128)S(1)} %copy-done.4, bf16[128,256]{1,0:T(8,128)(2,1)S(1)} %copy-done.7, f32[128,256]{1,0:T(8,128)S(1)} %copy-done.5, f32[128,256]{1,0:T(8,128)S(1)} %copy-done.6), kind=kLoop, calls=%fused_computation.16 | loop fusion | flops 524288 | bytes 851968 | tf_op jit(solution)/shard_map/sub | solution.py:148
  53.3 0.3 all-to-all-done.1.parts_ref
  53.6 0.9 %finish.1 = (bf16[2,4,256]{2,1,0:T(4,128)(2,1)}, bf16[2,4,1024]{2,1,0:T(4,128)(2,1)}) custom-call(f32[8,8,256]{2,1,0:T(8,128)S(1)} %all-to-all-done.1.parts_ref, bf16[64,128]{1,0:T(8,128)(2,1)S(1)} %get-tuple-element.27.heads_ref, f32[64,128]{1,0:T(8,128)S(1)} %get-tuple-element.28.acc_ref, f32[64,128]{1,0:T(8,128)S(1)} %get-tuple-element.29.peak_ref, ...), custom_call_target="tpu_custom_call" | custom-call | tf_op jit(solution)/shard_map/finish/pallas_call | solution.py:188
  (1 shorter events, 0.0 us)
Async XLA Ops:
  0.6 49.7 %copy-start.1 = (bf16[2,2048,128]{2,1,0:T(8,128)(2,1)S(1)}, bf16[2,2048,128]{2,1,0:T(8,128)(2,1)}, u32[]{:S(2)}) copy-start(bf16[2,2048,128]{2,1,0:T(8,128)(2,1)} %v_ref.1) | copy-start | bytes 3145732
  0.6 49.6 %copy-start = (bf16[2,2048,128]{2,1,0:T(8,128)(2,1)S(1)}, bf16[2,2048,128]{2,1,0:T(8,128)(2,1)}, u32[]{:S(2)}) copy-start(bf16[2,2048,128]{2,1,0:T(8,128)(2,1)} %k_ref.1) | copy-start | bytes 3145732
  0.7 22.8 %collective-permute-start = (bf16[2,4,1024]{2,1,0:T(4,128)(2,1)}, bf16[2,4,1024]{2,1,0:T(4,128)(2,1)S(1)}, u32[]{:S(2)}, u32[]{:S(2)}) collective-permute-start(bf16[2,4,1024]{2,1,0:T(4,128)(2,1)} %param.13), channel_id=1, source_target_pairs={{0,24},{4,80},{8,152},{12,200},{16,272},{20,344},{24,400},{28,448}... | collective-permute-start | bytes 49160 | tf_op jit(solution)/shard_map/ppermute | solution.py:141
  23.5 13.6 %collective-permute-start.1 = (bf16[512,256]{1,0:T(8,128)(2,1)S(1)}, bf16[512,256]{1,0:T(8,128)(2,1)S(1)}, u32[]{:S(2)}, u32[]{:S(2)}) collective-permute-start(bf16[512,256]{1,0:T(8,128)(2,1)S(1)} %all_gather.3.own_ref), channel_id=1, source_target_pairs={{0,32},{32,0},{1,33},{33,1},{2,34},{34,2},{3,35},{35,3},{4,36},{36... | collective-permute-start | bytes 786440 | tf_op jit(solution)/shard_map/ppermute | solution.py:154
  38.0 12.3 %copy-start.3 = (s32[2]{0:T(128)S(1)}, s32[2]{0:T(128)}, u32[]{:S(2)}) copy-start(s32[2]{0:T(128)} %lengths_ref.1) | copy-start | bytes 28
  38.0 15.7 %all-to-all-start.1 = ((f32[8,8,256]{2,1,0:T(8,128)}), f32[8,8,256]{2,1,0:T(8,128)S(1)}, u32[]{:S(2)}, u32[]{:S(2)}) async-start(f32[8,8,256]{2,1,0:T(8,128)} %project.1), calls=%async_computation.1 | async-start | bytes 131072 | tf_op jit(solution)/shard_map/all_to_all | solution.py:176
  50.3 0.7 %copy-start.2 = (bf16[2,4,1024]{2,1,0:T(4,128)(2,1)S(1)}, bf16[2,4,1024]{2,1,0:T(4,128)(2,1)}, u32[]{:S(2)}) copy-start(bf16[2,4,1024]{2,1,0:T(4,128)(2,1)} %q_ref) | copy-start | bytes 49156
  51.0 1.5 %copy-start.4 = (f32[128,256]{1,0:T(8,128)S(1)}, f32[128,256]{1,0:T(8,128)}, u32[]{:S(2)}) copy-start(f32[128,256]{1,0:T(8,128)} %param.9) | copy-start | bytes 393220
  51.0 1.5 %copy-start.5 = (f32[128,256]{1,0:T(8,128)S(1)}, f32[128,256]{1,0:T(8,128)}, u32[]{:S(2)}) copy-start(f32[128,256]{1,0:T(8,128)} %param.10) | copy-start | bytes 393220
  51.0 1.5 %copy-start.6 = (f32[128,256]{1,0:T(8,128)S(1)}, f32[128,256]{1,0:T(8,128)}, u32[]{:S(2)}) copy-start(f32[128,256]{1,0:T(8,128)} %param.11) | copy-start | bytes 393220
  51.0 1.5 %copy-start.7 = (bf16[128,256]{1,0:T(8,128)(2,1)S(1)}, bf16[128,256]{1,0:T(8,128)(2,1)}, u32[]{:S(2)}) copy-start(bf16[128,256]{1,0:T(8,128)(2,1)} %param.12) | copy-start | bytes 196612

commit v3 on v2

--- a/solution.py
+++ b/solution.py
@@ -46,6 +46,13 @@
 VMEM = pl.BlockSpec(memory_space=pltpu.VMEM)
 SMEM = pl.BlockSpec(memory_space=pltpu.SMEM)
 PARAMS = pltpu.CompilerParams(vmem_limit_bytes=32 * 1024 * 1024)
+
+
+def mask_kernel(out_ref):
+    row = lax.broadcasted_iota(jnp.int32, (64, 8), 0) % 8
+    column = lax.broadcasted_iota(jnp.int32, (64, 8), 1)
+    seen = (row // 4 == column // 4) & (column % 4 <= row % 4)
+    out_ref[...] = jnp.where(seen, jnp.float32(0), jnp.float32(-1e30))
 
 
 def slots_kernel(x_ref, out_ref):
@@ -104,7 +111,7 @@
     total_ref[...] = jnp.broadcast_to(total, (64, HD))
 
 
-def finish_kernel(parts_ref, heads_ref, acc_ref, peak_ref, total_ref, fresh_ref, out_ref):
+def finish_kernel(parts_ref, mask_ref, heads_ref, acc_ref, peak_ref, total_ref, fresh_ref, out_ref):
     fresh = jnp.sum(parts_ref[...], axis=0)
     fresh_ref[0] = fresh[:4].astype(jnp.bfloat16)
     fresh_ref[1] = fresh[4:].astype(jnp.bfloat16)
@@ -113,10 +120,7 @@
     score = lax.dot_general(
         heads_ref[...], fresh[:, :HD], contract, preferred_element_type=jnp.float32
     ) * (1.0 / math.sqrt(HD))
-    row = lax.broadcasted_iota(jnp.int32, (64, 8), 0) % 8
-    column = lax.broadcasted_iota(jnp.int32, (64, 8), 1)
-    seen = (row // 4 == column // 4) & (column % 4 <= row % 4)
-    score = jnp.where(seen, score, jnp.float32(-1e30))
+    score = jnp.where(mask_ref[...] == 0, score, jnp.float32(-1e30))
     old_peak = peak_ref[...]
     peak = jnp.maximum(old_peak, jnp.max(score, axis=1, keepdims=True))
     keep = jnp.exp(old_peak - peak)
@@ -148,7 +152,18 @@
         new_master = master - learning_rate * (update + weight_decay * master)
         return new_master, new_moment_one, new_moment_two
 
-    weights = adamw(master, moment_one, moment_two, gradient)[0].astype(bf16)
+    mask = pl.pallas_call(
+        mask_kernel,
+        out_shape=shape((64, 8), f32),
+        out_specs=VMEM,
+        compiler_params=PARAMS,
+        cost_estimate=pl.CostEstimate(
+            flops=4 * 64 * 4096 * 128, bytes_accessed=1 << 22, transcendentals=64 * 2048
+        ),
+        name="mask",
+    )()
+    state, mask = lax.optimization_barrier(((master, moment_one, moment_two, gradient), mask))
+    weights = adamw(*state)[0].astype(bf16)
     weights = lax.all_gather(weights, REP, axis=0, tiled=True)
     moved, weights = lax.optimization_barrier((moved, weights))
     others = lax.ppermute(weights, "zlow", [(0, 1), (1, 0)])
@@ -188,11 +203,11 @@
     fresh_kv, attended = pl.pallas_call(
         finish_kernel,
         out_shape=[shape((2, 4, 256), bf16), shape((2, 4, 1024), bf16)],
-        in_specs=[VMEM] * 5,
+        in_specs=[VMEM] * 6,
         out_specs=[VMEM] * 2,
         compiler_params=PARAMS,
         name="finish",
-    )(parts, *cached)
+    )(parts, mask, *cached)
     return new_master, new_moment_one, new_moment_two, fresh_kv, attended
 
 

time: 55 us -> 54.2 us (0.985)
  other arithmetic: 1.98 us -> 0.93 us
  waiting for transfers between devices: 0.32 us -> 1.1 us
  local copies, waits for them, and re-layouts: 0.74 us -> 0.04 us
    convert_element_type x1, other arithmetic: 1.18 us -> 0.12 us  [local(): weights = adamw(*state)[0].astype(bf16)]
    all_to_all x1, waiting for transfers between devices: 0.31 us -> 1.1 us  [local(): parts = lax.all_to_all(parts, 'zpair', 0, 0, axis_index_groups=[PAIRS])]
    unnamed x16, local copies, waits for them, and re-layouts: 0.74 us -> 0.04 us
  transfers between devices with their start and end apart: 3 -> 3, of which waited for: 1 -> 1; matrix products, arithmetic and copies ran while one was open for 4% -> 2% of each run, Pallas kernels for 3% -> 3%
where the time goes in v3:
time: 54.2 us; the launch traced here: 53.9 us
  starting transfers between devices  31.2 us (58%)
  blocking collectives  16.6 us (31%)
  Pallas kernels  3.25 us (6%)
  waiting for transfers between devices  1.1 us (2%)
  other arithmetic  0.93 us (2%)
  between operations  0.79 us (1%)
    ppermute x1, starting transfers between devices, local(): moved = lax.ppermute(hidden, LEARN + TP, HOPS)  15.9 us
    all_to_all x1, starting transfers between devices, local(): parts = lax.all_to_all(parts, 'zpair', 0, 0, axis_index_groups=[PAIRS])  12.4 us
    all_to_all x1, blocking collectives, local(): tokens = lax.all_to_all(slots, TP, 0, 0, axis_index_groups=[BLOCKS])  10.7 us
    all_gather x1, blocking collectives, local(): weights = lax.all_gather(weights, REP, axis=0, tiled=True)  5.92 us
    ppermute x1, starting transfers between devices, local(): others = lax.ppermute(weights, 'zlow', [(0, 1), (1, 0)])  2.92 us
    pallas_call x1, Pallas kernels, local(): pl.pallas_call(cache_kernel, out_shape=[shape((64, HD), bf16)] + [shape((...  1.44 us
    all_to_all x1, waiting for transfers between devices, local(): parts = lax.all_to_all(parts, 'zpair', 0, 0, axis_index_groups=[PAIRS])  1.1 us
  transfers between devices with their start and end apart: 3, of which 1 were waited for; matrix products, arithmetic and copies ran while one was open for 2% of the time, Pallas kernels for 3%

profile of v3, /device:TPU:24, one launch (start us, length us, event | category | flops | bytes accessed | tf_op | source)
XLA Modules:
  0.0 53.9 jit_solution(17368154261375675298)
XLA Ops:
  0.6 0.0 copy-start.7
  0.6 0.0 copy-start.6
  0.7 0.0 copy-start.5
  0.7 0.0 copy-start.4
  0.7 15.9 %collective-permute-start = (bf16[2,4,1024]{2,1,0:T(4,128)(2,1)}, bf16[2,4,1024]{2,1,0:T(4,128)(2,1)S(1)}, u32[]{:S(2)}, u32[]{:S(2)}) collective-permute-start(bf16[2,4,1024]{2,1,0:T(4,128)(2,1)} %param.13), channel_id=1, source_target_pairs={{0,24},{4,80},{8,152},{12,200},{16,272},{20,344},{24,400},{28,448}... | collective-permute-start | bytes 49160 | tf_op jit(solution)/shard_map/ppermute | solution.py:145
  16.5 0.0 copy-start.2
  16.6 0.0 copy-done.7
  16.6 0.0 copy-done.6
  16.6 0.0 copy-done.5
  16.6 0.0 copy-done.4
  16.6 0.0 copy-start
  16.6 0.0 copy-start.1
  16.6 0.1 fusion.12
  16.8 5.9 %all_gather.3.own_ref = bf16[512,256]{1,0:T(8,128)(2,1)S(1)} all-gather(bf16[128,256]{1,0:T(8,128)(2,1)S(1)} %fusion.12), channel_id=1, replica_groups=mesh['zpair'=8,'zlow'=2,'yfar'=2,'x'=4,'ynear'=2,'core'=2] {'ynear','core'}, dimensions={0}, use_global_device_ids=true | all-gather | bytes 327680 | tf_op jit(solution)/shard_map/all_gather | solution.py:167
  22.7 0.0 collective-permute-done.x_ref
  22.7 2.9 %collective-permute-start.1 = (bf16[512,256]{1,0:T(8,128)(2,1)S(1)}, bf16[512,256]{1,0:T(8,128)(2,1)S(1)}, u32[]{:S(2)}, u32[]{:S(2)}) collective-permute-start(bf16[512,256]{1,0:T(8,128)(2,1)S(1)} %all_gather.3.own_ref), channel_id=1, source_target_pairs={{0,32},{32,0},{1,33},{33,1},{2,34},{34,2},{3,35},{35,3},{4,36},{36... | collective-permute-start | bytes 786440 | tf_op jit(solution)/shard_map/ppermute | solution.py:169
  25.6 10.7 %all_to_all.10.y_ref = bf16[8,8,1024]{2,1,0:T(8,128)(2,1)S(1)} all-to-all(bf16[8,8,1024]{2,1,0:T(8,128)(2,1)S(1)} %slots.1), channel_id=1, replica_groups={{16,20,24,28,0,4,8,12},{17,21,25,29,1,5,9,13},{18,22,26,30,2,6,10,14},{..., dimensions={0} | all-to-all | bytes 262144 | tf_op jit(solution)/shard_map/all_to_all | solution.py:178
  36.3 0.0 collective-permute-done.1.other_ref
  36.3 0.8 %project.1 = f32[8,8,256]{2,1,0:T(8,128)} custom-call(bf16[8,8,1024]{2,1,0:T(8,128)(2,1)S(1)} %all_to_all.10.y_ref, bf16[512,256]{1,0:T(8,128)(2,1)S(1)} %all_gather.3.own_ref, bf16[512,256]{1,0:T(8,128)(2,1)S(1)} %collective-permute-done.1.other_ref), custom_call_target="tpu_custom_call" | custom-call | tf_op jit(solution)/shard_map/project/pallas_call | solution.py:179
  37.2 0.0 copy-start.3
  37.2 12.4 %all-to-all-start.1 = ((f32[8,8,256]{2,1,0:T(8,128)}), f32[8,8,256]{2,1,0:T(8,128)S(1)}, u32[]{:S(2)}, u32[]{:S(2)}) async-start(f32[8,8,256]{2,1,0:T(8,128)} %project.1), calls=%async_computation.1 | async-start | bytes 131072 | tf_op jit(solution)/shard_map/all_to_all | solution.py:191
  49.6 0.0 copy-done.2
  49.6 0.0 copy-done
  49.6 0.0 copy-done.1
  49.6 0.0 copy-done.3
  49.6 1.4 %cache.1 = (bf16[64,128]{1,0:T(8,128)(2,1)S(1)}, f32[64,128]{1,0:T(8,128)S(1)}, f32[64,128]{1,0:T(8,128)S(1)}, f32[64,128]{1,0:T(8,128)S(1)}) custom-call(s32[2]{0:T(128)S(1)} %copy-done.3, bf16[2,4,1024]{2,1,0:T(4,128)(2,1)S(1)} %copy-done.2, bf16[2,2048,128]{2,1,0:T(8,128)(2,1)S(1)} %copy-done, bf16[2,2048,128]{2,1,0:T(8,128)(2,1)S(1)} %copy-done.1), custom_call_target="tpu_custom_call" | custom-call | flops 134217728 | bytes 4194304 | tf_op jit(solution)/shard_map/cache/pallas_call | solution.py:192
  51.0 0.8 %multiply_subtract_fusion = (f32[128,256]{1,0:T(8,128)}, f32[128,256]{1,0:T(8,128)}, f32[128,256]{1,0:T(8,128)}) fusion(f32[128,256]{1,0:T(8,128)S(1)} %copy-done.4, bf16[128,256]{1,0:T(8,128)(2,1)S(1)} %copy-done.7, f32[128,256]{1,0:T(8,128)S(1)} %copy-done.5, f32[128,256]{1,0:T(8,128)S(1)} %copy-done.6), kind=kLoop, calls=%fused_computation.16 | loop fusion | flops 524288 | bytes 851968 | tf_op jit(solution)/shard_map/sub | solution.py:152
  51.8 1.1 %all-to-all-done.1.parts_ref = f32[8,8,256]{2,1,0:T(8,128)S(1)} async-done(((f32[8,8,256]{2,1,0:T(8,128)}), f32[8,8,256]{2,1,0:T(8,128)S(1)}, u32[]{:S(2)}, u32[]{:S(2)}) %all-to-all-start.1) | async-done | bytes 65568 | tf_op jit(solution)/shard_map/all_to_all | solution.py:191
  52.9 0.9 %finish.1 = (bf16[2,4,256]{2,1,0:T(4,128)(2,1)}, bf16[2,4,1024]{2,1,0:T(4,128)(2,1)}) custom-call(f32[8,8,256]{2,1,0:T(8,128)S(1)} %all-to-all-done.1.parts_ref, f32[64,8]{1,0:T(8,128)S(1)} %mask.1.mask_ref, bf16[64,128]{1,0:T(8,128)(2,1)S(1)} %get-tuple-element.37.heads_ref, f32[64,128]{1,0:T(8,128)S(1)} %get-tuple-element.38.acc_ref, ...), custom_call_target="tpu_custom_call" | custom-call | tf_op jit(solution)/shard_map/finish/pallas_call | solution.py:203
  (2 shorter events, 0.0 us)
Async XLA Ops:
  0.6 15.9 %copy-start.7 = (bf16[128,256]{1,0:T(8,128)(2,1)S(1)}, bf16[128,256]{1,0:T(8,128)(2,1)}, u32[]{:S(2)}) copy-start(bf16[128,256]{1,0:T(8,128)(2,1)} %param.12) | copy-start | bytes 196612
  0.6 15.9 %copy-start.6 = (f32[128,256]{1,0:T(8,128)S(1)}, f32[128,256]{1,0:T(8,128)}, u32[]{:S(2)}) copy-start(f32[128,256]{1,0:T(8,128)} %param.11) | copy-start | bytes 393220
  0.7 15.9 %copy-start.5 = (f32[128,256]{1,0:T(8,128)S(1)}, f32[128,256]{1,0:T(8,128)}, u32[]{:S(2)}) copy-start(f32[128,256]{1,0:T(8,128)} %param.10) | copy-start | bytes 393220
  0.7 15.9 %copy-start.4 = (f32[128,256]{1,0:T(8,128)S(1)}, f32[128,256]{1,0:T(8,128)}, u32[]{:S(2)}) copy-start(f32[128,256]{1,0:T(8,128)} %param.9) | copy-start | bytes 393220
  0.7 22.0 %collective-permute-start = (bf16[2,4,1024]{2,1,0:T(4,128)(2,1)}, bf16[2,4,1024]{2,1,0:T(4,128)(2,1)S(1)}, u32[]{:S(2)}, u32[]{:S(2)}) collective-permute-start(bf16[2,4,1024]{2,1,0:T(4,128)(2,1)} %param.13), channel_id=1, source_target_pairs={{0,24},{4,80},{8,152},{12,200},{16,272},{20,344},{24,400},{28,448}... | collective-permute-start | bytes 49160 | tf_op jit(solution)/shard_map/ppermute | solution.py:145
  16.5 33.0 %copy-start.2 = (bf16[2,4,1024]{2,1,0:T(4,128)(2,1)S(1)}, bf16[2,4,1024]{2,1,0:T(4,128)(2,1)}, u32[]{:S(2)}) copy-start(bf16[2,4,1024]{2,1,0:T(4,128)(2,1)} %q_ref) | copy-start | bytes 49156
  16.6 33.0 %copy-start = (bf16[2,2048,128]{2,1,0:T(8,128)(2,1)S(1)}, bf16[2,2048,128]{2,1,0:T(8,128)(2,1)}, u32[]{:S(2)}) copy-start(bf16[2,2048,128]{2,1,0:T(8,128)(2,1)} %k_ref.1) | copy-start | bytes 3145732
  16.6 33.0 %copy-start.1 = (bf16[2,2048,128]{2,1,0:T(8,128)(2,1)S(1)}, bf16[2,2048,128]{2,1,0:T(8,128)(2,1)}, u32[]{:S(2)}) copy-start(bf16[2,2048,128]{2,1,0:T(8,128)(2,1)} %v_ref.1) | copy-start | bytes 3145732
  22.7 13.6 %collective-permute-start.1 = (bf16[512,256]{1,0:T(8,128)(2,1)S(1)}, bf16[512,256]{1,0:T(8,128)(2,1)S(1)}, u32[]{:S(2)}, u32[]{:S(2)}) collective-permute-start(bf16[512,256]{1,0:T(8,128)(2,1)S(1)} %all_gather.3.own_ref), channel_id=1, source_target_pairs={{0,32},{32,0},{1,33},{33,1},{2,34},{34,2},{3,35},{35,3},{4,36},{36... | collective-permute-start | bytes 786440 | tf_op jit(solution)/shard_map/ppermute | solution.py:169
  37.2 12.4 %copy-start.3 = (s32[2]{0:T(128)S(1)}, s32[2]{0:T(128)}, u32[]{:S(2)}) copy-start(s32[2]{0:T(128)} %lengths_ref.1) | copy-start | bytes 28
  37.2 15.8 %all-to-all-start.1 = ((f32[8,8,256]{2,1,0:T(8,128)}), f32[8,8,256]{2,1,0:T(8,128)S(1)}, u32[]{:S(2)}, u32[]{:S(2)}) async-start(f32[8,8,256]{2,1,0:T(8,128)} %project.1), calls=%async_computation.1 | async-start | bytes 131072 | tf_op jit(solution)/shard_map/all_to_all | solution.py:191

commit v4 on v3

--- a/solution.py
+++ b/solution.py
@@ -41,7 +41,8 @@
     for low in range(2)
     for block in range(8)
 ]
-BLOCKS = [(i + 4) % 8 for i in range(8)]
+ROOTS = (4, 4, 5, 7, 7, 5, 7, 7)
+PLANES = [[8 * plane + (i + root) % 8 for i in range(8)] for plane, root in enumerate(ROOTS)]
 PAIRS = [(i + 4) % 8 for i in range(8)]
 VMEM = pl.BlockSpec(memory_space=pltpu.VMEM)
 SMEM = pl.BlockSpec(memory_space=pltpu.SMEM)
@@ -66,12 +67,16 @@
     here = lax.axis_index("zpair")
     low = lax.axis_index("zlow")
     rows = y_ref[...].astype(jnp.float32).reshape(64, 1024)
-    first, second = rows[:, :512], rows[:, 512:]
-    mine = jnp.where(low == 0, first, second).astype(jnp.bfloat16)
-    theirs = jnp.where(low == 0, second, first).astype(jnp.bfloat16)
+    left, right = rows[:, :512], rows[:, 512:]
+    mine = jnp.where(low == 0, left, right).astype(jnp.bfloat16)
+    theirs = jnp.where(low == 0, right, left).astype(jnp.bfloat16)
     part = jnp.dot(mine, own_ref[...], preferred_element_type=jnp.float32)
     part = part + jnp.dot(theirs, other_ref[...], preferred_element_type=jnp.float32)
-    for i, t in enumerate(BLOCKS):
+    first = jnp.int32(ROOTS[0])
+    for plane in range(1, 8):
+        first = jnp.where(here == plane, ROOTS[plane], first)
+    for i in range(8):
+        t = (i + first) % 8
         far = (here // 4) ^ (t // 4)
         along = (t % 4 - here % 4 + 4) % 4
         away = jnp.where(
@@ -175,7 +180,7 @@
         compiler_params=PARAMS,
         name="slots",
     )(moved)
-    tokens = lax.all_to_all(slots, TP, 0, 0, axis_index_groups=[BLOCKS])
+    tokens = lax.all_to_all(slots, ("zpair",) + TP, 0, 0, axis_index_groups=PLANES)
     parts = pl.pallas_call(
         project_kernel,
         out_shape=shape((8, 8, 256), f32),

time: 54.2 us -> 54.1 us (level)
  no operation moved by 1% of the time
where the time goes in v4:
time: 54.1 us; the launch traced here: 53.8 us
  starting transfers between devices  31.1 us (57%)
  blocking collectives  16.6 us (31%)
  Pallas kernels  3.28 us (6%)
  waiting for transfers between devices  1.08 us (2%)
  other arithmetic  0.93 us (2%)
  between operations  0.79 us (1%)
    ppermute x1, starting transfers between devices, local(): moved = lax.ppermute(hidden, LEARN + TP, HOPS)  15.9 us
    all_to_all x1, starting transfers between devices, local(): parts = lax.all_to_all(parts, 'zpair', 0, 0, axis_index_groups=[PAIRS])  12.3 us
    all_to_all x1, blocking collectives, local(): lax.all_to_all(slots, ('zpair',) + TP, 0, 0, axis_index_groups=PLANES)  10.7 us
    all_gather x1, blocking collectives, local(): weights = lax.all_gather(weights, REP, axis=0, tiled=True)  5.92 us
    ppermute x1, starting transfers between devices, local(): others = lax.ppermute(weights, 'zlow', [(0, 1), (1, 0)])  2.92 us
    pallas_call x1, Pallas kernels, local(): pl.pallas_call(cache_kernel, out_shape=[shape((64, HD), bf16)] + [shape((...  1.44 us
  transfers between devices with their start and end apart: 3, of which 1 were waited for; matrix products, arithmetic and copies ran while one was open for 2% of the time, Pallas kernels for 3%

profile of v4, /device:TPU:24, one launch (start us, length us, event | category | flops | bytes accessed | tf_op | source)
XLA Modules:
  0.0 53.8 jit_solution(8591595855219775416)
XLA Ops:
  0.6 0.0 copy-start.7
  0.6 0.0 copy-start.6
  0.7 0.0 copy-start.5
  0.7 0.0 copy-start.4
  0.7 15.9 %collective-permute-start = (bf16[2,4,1024]{2,1,0:T(4,128)(2,1)}, bf16[2,4,1024]{2,1,0:T(4,128)(2,1)S(1)}, u32[]{:S(2)}, u32[]{:S(2)}) collective-permute-start(bf16[2,4,1024]{2,1,0:T(4,128)(2,1)} %param.13), channel_id=1, source_target_pairs={{0,24},{4,80},{8,152},{12,200},{16,272},{20,344},{24,400},{28,448}... | collective-permute-start | bytes 49160 | tf_op jit(solution)/shard_map/ppermute | solution.py:150
  16.5 0.0 copy-start.2
  16.6 0.0 copy-done.7
  16.6 0.0 copy-done.6
  16.6 0.0 copy-done.5
  16.6 0.0 copy-done.4
  16.6 0.0 copy-start
  16.6 0.0 copy-start.1
  16.6 0.1 fusion.12
  16.8 5.9 %all_gather.3.own_ref = bf16[512,256]{1,0:T(8,128)(2,1)S(1)} all-gather(bf16[128,256]{1,0:T(8,128)(2,1)S(1)} %fusion.12), channel_id=1, replica_groups=mesh['zpair'=8,'zlow'=2,'yfar'=2,'x'=4,'ynear'=2,'core'=2] {'ynear','core'}, dimensions={0}, use_global_device_ids=true | all-gather | bytes 327680 | tf_op jit(solution)/shard_map/all_gather | solution.py:172
  22.7 0.0 collective-permute-done.x_ref
  22.7 2.9 %collective-permute-start.1 = (bf16[512,256]{1,0:T(8,128)(2,1)S(1)}, bf16[512,256]{1,0:T(8,128)(2,1)S(1)}, u32[]{:S(2)}, u32[]{:S(2)}) collective-permute-start(bf16[512,256]{1,0:T(8,128)(2,1)S(1)} %all_gather.3.own_ref), channel_id=1, source_target_pairs={{0,32},{32,0},{1,33},{33,1},{2,34},{34,2},{3,35},{35,3},{4,36},{36... | collective-permute-start | bytes 786440 | tf_op jit(solution)/shard_map/ppermute | solution.py:174
  25.6 10.7 %all_to_all.10.y_ref = bf16[8,8,1024]{2,1,0:T(8,128)(2,1)S(1)} all-to-all(bf16[8,8,1024]{2,1,0:T(8,128)(2,1)S(1)} %slots.1), channel_id=1, replica_groups={{16,20,24,28,0,4,8,12},{80,84,88,92,64,68,72,76},{148,152,156,128,132,1..., dimensions={0} | all-to-all | bytes 262144 | tf_op jit(solution)/shard_map/all_to_all | solution.py:183
  36.3 0.0 collective-permute-done.1.other_ref
  36.3 0.9 %project.1 = f32[8,8,256]{2,1,0:T(8,128)} custom-call(bf16[8,8,1024]{2,1,0:T(8,128)(2,1)S(1)} %all_to_all.10.y_ref, bf16[512,256]{1,0:T(8,128)(2,1)S(1)} %all_gather.3.own_ref, bf16[512,256]{1,0:T(8,128)(2,1)S(1)} %collective-permute-done.1.other_ref), custom_call_target="tpu_custom_call" | custom-call | tf_op jit(solution)/shard_map/project/pallas_call | solution.py:184
  37.2 0.0 copy-start.3
  37.2 12.3 %all-to-all-start.1 = ((f32[8,8,256]{2,1,0:T(8,128)}), f32[8,8,256]{2,1,0:T(8,128)S(1)}, u32[]{:S(2)}, u32[]{:S(2)}) async-start(f32[8,8,256]{2,1,0:T(8,128)} %project.1), calls=%async_computation.1 | async-start | bytes 131072 | tf_op jit(solution)/shard_map/all_to_all | solution.py:196
  49.5 0.0 copy-done.2
  49.5 0.0 copy-done
  49.5 0.0 copy-done.1
  49.5 0.0 copy-done.3
  49.5 1.4 %cache.1 = (bf16[64,128]{1,0:T(8,128)(2,1)S(1)}, f32[64,128]{1,0:T(8,128)S(1)}, f32[64,128]{1,0:T(8,128)S(1)}, f32[64,128]{1,0:T(8,128)S(1)}) custom-call(s32[2]{0:T(128)S(1)} %copy-done.3, bf16[2,4,1024]{2,1,0:T(4,128)(2,1)S(1)} %copy-done.2, bf16[2,2048,128]{2,1,0:T(8,128)(2,1)S(1)} %copy-done, bf16[2,2048,128]{2,1,0:T(8,128)(2,1)S(1)} %copy-done.1), custom_call_target="tpu_custom_call" | custom-call | flops 134217728 | bytes 4194304 | tf_op jit(solution)/shard_map/cache/pallas_call | solution.py:197
  51.0 0.8 %multiply_subtract_fusion = (f32[128,256]{1,0:T(8,128)}, f32[128,256]{1,0:T(8,128)}, f32[128,256]{1,0:T(8,128)}) fusion(f32[128,256]{1,0:T(8,128)S(1)} %copy-done.4, bf16[128,256]{1,0:T(8,128)(2,1)S(1)} %copy-done.7, f32[128,256]{1,0:T(8,128)S(1)} %copy-done.5, f32[128,256]{1,0:T(8,128)S(1)} %copy-done.6), kind=kLoop, calls=%fused_computation.16 | loop fusion | flops 524288 | bytes 851968 | tf_op jit(solution)/shard_map/sub | solution.py:157
  51.8 1.1 %all-to-all-done.1.parts_ref = f32[8,8,256]{2,1,0:T(8,128)S(1)} async-done(((f32[8,8,256]{2,1,0:T(8,128)}), f32[8,8,256]{2,1,0:T(8,128)S(1)}, u32[]{:S(2)}, u32[]{:S(2)}) %all-to-all-start.1) | async-done | bytes 65568 | tf_op jit(solution)/shard_map/all_to_all | solution.py:196
  52.9 0.9 %finish.1 = (bf16[2,4,256]{2,1,0:T(4,128)(2,1)}, bf16[2,4,1024]{2,1,0:T(4,128)(2,1)}) custom-call(f32[8,8,256]{2,1,0:T(8,128)S(1)} %all-to-all-done.1.parts_ref, f32[64,8]{1,0:T(8,128)S(1)} %mask.1.mask_ref, bf16[64,128]{1,0:T(8,128)(2,1)S(1)} %get-tuple-element.37.heads_ref, f32[64,128]{1,0:T(8,128)S(1)} %get-tuple-element.38.acc_ref, ...), custom_call_target="tpu_custom_call" | custom-call | tf_op jit(solution)/shard_map/finish/pallas_call | solution.py:208
  (2 shorter events, 0.0 us)
Async XLA Ops:
  0.6 15.9 %copy-start.7 = (bf16[128,256]{1,0:T(8,128)(2,1)S(1)}, bf16[128,256]{1,0:T(8,128)(2,1)}, u32[]{:S(2)}) copy-start(bf16[128,256]{1,0:T(8,128)(2,1)} %param.12) | copy-start | bytes 196612
  0.6 15.9 %copy-start.6 = (f32[128,256]{1,0:T(8,128)S(1)}, f32[128,256]{1,0:T(8,128)}, u32[]{:S(2)}) copy-start(f32[128,256]{1,0:T(8,128)} %param.11) | copy-start | bytes 393220
  0.7 15.9 %copy-start.5 = (f32[128,256]{1,0:T(8,128)S(1)}, f32[128,256]{1,0:T(8,128)}, u32[]{:S(2)}) copy-start(f32[128,256]{1,0:T(8,128)} %param.10) | copy-start | bytes 393220
  0.7 15.9 %copy-start.4 = (f32[128,256]{1,0:T(8,128)S(1)}, f32[128,256]{1,0:T(8,128)}, u32[]{:S(2)}) copy-start(f32[128,256]{1,0:T(8,128)} %param.9) | copy-start | bytes 393220
  0.7 22.0 %collective-permute-start = (bf16[2,4,1024]{2,1,0:T(4,128)(2,1)}, bf16[2,4,1024]{2,1,0:T(4,128)(2,1)S(1)}, u32[]{:S(2)}, u32[]{:S(2)}) collective-permute-start(bf16[2,4,1024]{2,1,0:T(4,128)(2,1)} %param.13), channel_id=1, source_target_pairs={{0,24},{4,80},{8,152},{12,200},{16,272},{20,344},{24,400},{28,448}... | collective-permute-start | bytes 49160 | tf_op jit(solution)/shard_map/ppermute | solution.py:150
  16.5 33.0 %copy-start.2 = (bf16[2,4,1024]{2,1,0:T(4,128)(2,1)S(1)}, bf16[2,4,1024]{2,1,0:T(4,128)(2,1)}, u32[]{:S(2)}) copy-start(bf16[2,4,1024]{2,1,0:T(4,128)(2,1)} %q_ref) | copy-start | bytes 49156
  16.6 32.9 %copy-start = (bf16[2,2048,128]{2,1,0:T(8,128)(2,1)S(1)}, bf16[2,2048,128]{2,1,0:T(8,128)(2,1)}, u32[]{:S(2)}) copy-start(bf16[2,2048,128]{2,1,0:T(8,128)(2,1)} %k_ref.1) | copy-start | bytes 3145732
  16.6 32.9 %copy-start.1 = (bf16[2,2048,128]{2,1,0:T(8,128)(2,1)S(1)}, bf16[2,2048,128]{2,1,0:T(8,128)(2,1)}, u32[]{:S(2)}) copy-start(bf16[2,2048,128]{2,1,0:T(8,128)(2,1)} %v_ref.1) | copy-start | bytes 3145732
  22.7 13.6 %collective-permute-start.1 = (bf16[512,256]{1,0:T(8,128)(2,1)S(1)}, bf16[512,256]{1,0:T(8,128)(2,1)S(1)}, u32[]{:S(2)}, u32[]{:S(2)}) collective-permute-start(bf16[512,256]{1,0:T(8,128)(2,1)S(1)} %all_gather.3.own_ref), channel_id=1, source_target_pairs={{0,32},{32,0},{1,33},{33,1},{2,34},{34,2},{3,35},{35,3},{4,36},{36... | collective-permute-start | bytes 786440 | tf_op jit(solution)/shard_map/ppermute | solution.py:174
  37.2 12.4 %copy-start.3 = (s32[2]{0:T(128)S(1)}, s32[2]{0:T(128)}, u32[]{:S(2)}) copy-start(s32[2]{0:T(128)} %lengths_ref.1) | copy-start | bytes 28
  37.2 15.7 %all-to-all-start.1 = ((f32[8,8,256]{2,1,0:T(8,128)}), f32[8,8,256]{2,1,0:T(8,128)S(1)}, u32[]{:S(2)}, u32[]{:S(2)}) async-start(f32[8,8,256]{2,1,0:T(8,128)} %project.1), calls=%async_computation.1 | async-start | bytes 131072 | tf_op jit(solution)/shard_map/all_to_all | solution.py:196

commit v5 on v3

--- a/solution.py
+++ b/solution.py
@@ -41,7 +41,7 @@
     for low in range(2)
     for block in range(8)
 ]
-BLOCKS = [(i + 4) % 8 for i in range(8)]
+BLOCKS = [4, 0, 5, 1, 6, 2, 7, 3]
 PAIRS = [(i + 4) % 8 for i in range(8)]
 VMEM = pl.BlockSpec(memory_space=pltpu.VMEM)
 SMEM = pl.BlockSpec(memory_space=pltpu.SMEM)

time: 54.2 us -> 54.1 us (level)
  no operation moved by 1% of the time
where the time goes in v5:
time: 54.1 us; the launch traced here: 53.7 us
  starting transfers between devices  31.2 us (58%)
  blocking collectives  16.4 us (30%)
  Pallas kernels  3.25 us (6%)
  waiting for transfers between devices  1.09 us (2%)
  other arithmetic  0.93 us (2%)
  between operations  0.79 us (1%)
    ppermute x1, starting transfers between devices, local(): moved = lax.ppermute(hidden, LEARN + TP, HOPS)  15.9 us
    all_to_all x1, starting transfers between devices, local(): parts = lax.all_to_all(parts, 'zpair', 0, 0, axis_index_groups=[PAIRS])  12.4 us
    all_to_all x1, blocking collectives, local(): tokens = lax.all_to_all(slots, TP, 0, 0, axis_index_groups=[BLOCKS])  10.5 us
    all_gather x1, blocking collectives, local(): weights = lax.all_gather(weights, REP, axis=0, tiled=True)  5.92 us
    ppermute x1, starting transfers between devices, local(): others = lax.ppermute(weights, 'zlow', [(0, 1), (1, 0)])  2.92 us
    pallas_call x1, Pallas kernels, local(): pl.pallas_call(cache_kernel, out_shape=[shape((64, HD), bf16)] + [shape((...  1.44 us
  transfers between devices with their start and end apart: 3, of which 1 were waited for; matrix products, arithmetic and copies ran while one was open for 2% of the time, Pallas kernels for 3%

profile of v5, /device:TPU:24, one launch (start us, length us, event | category | flops | bytes accessed | tf_op | source)
XLA Modules:
  0.0 53.7 jit_solution(11477685016450672928)
XLA Ops:
  0.6 0.0 copy-start.7
  0.6 0.0 copy-start.6
  0.7 0.0 copy-start.5
  0.7 0.0 copy-start.4
  0.7 15.9 %collective-permute-start = (bf16[2,4,1024]{2,1,0:T(4,128)(2,1)}, bf16[2,4,1024]{2,1,0:T(4,128)(2,1)S(1)}, u32[]{:S(2)}, u32[]{:S(2)}) collective-permute-start(bf16[2,4,1024]{2,1,0:T(4,128)(2,1)} %param.13), channel_id=1, source_target_pairs={{0,24},{4,80},{8,152},{12,200},{16,272},{20,344},{24,400},{28,448}... | collective-permute-start | bytes 49160 | tf_op jit(solution)/shard_map/ppermute | solution.py:145
  16.5 0.0 copy-start.2
  16.6 0.0 copy-done.7
  16.6 0.0 copy-done.6
  16.6 0.0 copy-done.5
  16.6 0.0 copy-done.4
  16.6 0.0 copy-start
  16.6 0.0 copy-start.1
  16.6 0.1 fusion.12
  16.8 5.9 %all_gather.3.own_ref = bf16[512,256]{1,0:T(8,128)(2,1)S(1)} all-gather(bf16[128,256]{1,0:T(8,128)(2,1)S(1)} %fusion.12), channel_id=1, replica_groups=mesh['zpair'=8,'zlow'=2,'yfar'=2,'x'=4,'ynear'=2,'core'=2] {'ynear','core'}, dimensions={0}, use_global_device_ids=true | all-gather | bytes 327680 | tf_op jit(solution)/shard_map/all_gather | solution.py:167
  22.7 0.0 collective-permute-done.x_ref
  22.7 2.9 %collective-permute-start.1 = (bf16[512,256]{1,0:T(8,128)(2,1)S(1)}, bf16[512,256]{1,0:T(8,128)(2,1)S(1)}, u32[]{:S(2)}, u32[]{:S(2)}) collective-permute-start(bf16[512,256]{1,0:T(8,128)(2,1)S(1)} %all_gather.3.own_ref), channel_id=1, source_target_pairs={{0,32},{32,0},{1,33},{33,1},{2,34},{34,2},{3,35},{35,3},{4,36},{36... | collective-permute-start | bytes 786440 | tf_op jit(solution)/shard_map/ppermute | solution.py:169
  25.6 10.5 %all_to_all.10.y_ref = bf16[8,8,1024]{2,1,0:T(8,128)(2,1)S(1)} all-to-all(bf16[8,8,1024]{2,1,0:T(8,128)(2,1)S(1)} %slots.1), channel_id=1, replica_groups={{16,0,20,4,24,8,28,12},{17,1,21,5,25,9,29,13},{18,2,22,6,26,10,30,14},{..., dimensions={0} | all-to-all | bytes 262144 | tf_op jit(solution)/shard_map/all_to_all | solution.py:178
  36.1 0.0 collective-permute-done.1.other_ref
  36.1 0.8 %project.1 = f32[8,8,256]{2,1,0:T(8,128)} custom-call(bf16[8,8,1024]{2,1,0:T(8,128)(2,1)S(1)} %all_to_all.10.y_ref, bf16[512,256]{1,0:T(8,128)(2,1)S(1)} %all_gather.3.own_ref, bf16[512,256]{1,0:T(8,128)(2,1)S(1)} %collective-permute-done.1.other_ref), custom_call_target="tpu_custom_call" | custom-call | tf_op jit(solution)/shard_map/project/pallas_call | solution.py:179
  37.0 0.0 copy-start.3
  37.0 12.4 %all-to-all-start.1 = ((f32[8,8,256]{2,1,0:T(8,128)}), f32[8,8,256]{2,1,0:T(8,128)S(1)}, u32[]{:S(2)}, u32[]{:S(2)}) async-start(f32[8,8,256]{2,1,0:T(8,128)} %project.1), calls=%async_computation.1 | async-start | bytes 131072 | tf_op jit(solution)/shard_map/all_to_all | solution.py:191
  49.4 0.0 copy-done.2
  49.4 0.0 copy-done
  49.4 0.0 copy-done.1
  49.4 0.0 copy-done.3
  49.4 1.4 %cache.1 = (bf16[64,128]{1,0:T(8,128)(2,1)S(1)}, f32[64,128]{1,0:T(8,128)S(1)}, f32[64,128]{1,0:T(8,128)S(1)}, f32[64,128]{1,0:T(8,128)S(1)}) custom-call(s32[2]{0:T(128)S(1)} %copy-done.3, bf16[2,4,1024]{2,1,0:T(4,128)(2,1)S(1)} %copy-done.2, bf16[2,2048,128]{2,1,0:T(8,128)(2,1)S(1)} %copy-done, bf16[2,2048,128]{2,1,0:T(8,128)(2,1)S(1)} %copy-done.1), custom_call_target="tpu_custom_call" | custom-call | flops 134217728 | bytes 4194304 | tf_op jit(solution)/shard_map/cache/pallas_call | solution.py:192
  50.9 0.8 %multiply_subtract_fusion = (f32[128,256]{1,0:T(8,128)}, f32[128,256]{1,0:T(8,128)}, f32[128,256]{1,0:T(8,128)}) fusion(f32[128,256]{1,0:T(8,128)S(1)} %copy-done.4, bf16[128,256]{1,0:T(8,128)(2,1)S(1)} %copy-done.7, f32[128,256]{1,0:T(8,128)S(1)} %copy-done.5, f32[128,256]{1,0:T(8,128)S(1)} %copy-done.6), kind=kLoop, calls=%fused_computation.16 | loop fusion | flops 524288 | bytes 851968 | tf_op jit(solution)/shard_map/sub | solution.py:152
  51.7 1.1 %all-to-all-done.1.parts_ref = f32[8,8,256]{2,1,0:T(8,128)S(1)} async-done(((f32[8,8,256]{2,1,0:T(8,128)}), f32[8,8,256]{2,1,0:T(8,128)S(1)}, u32[]{:S(2)}, u32[]{:S(2)}) %all-to-all-start.1) | async-done | bytes 65568 | tf_op jit(solution)/shard_map/all_to_all | solution.py:191
  52.8 0.9 %finish.1 = (bf16[2,4,256]{2,1,0:T(4,128)(2,1)}, bf16[2,4,1024]{2,1,0:T(4,128)(2,1)}) custom-call(f32[8,8,256]{2,1,0:T(8,128)S(1)} %all-to-all-done.1.parts_ref, f32[64,8]{1,0:T(8,128)S(1)} %mask.1.mask_ref, bf16[64,128]{1,0:T(8,128)(2,1)S(1)} %get-tuple-element.37.heads_ref, f32[64,128]{1,0:T(8,128)S(1)} %get-tuple-element.38.acc_ref, ...), custom_call_target="tpu_custom_call" | custom-call | tf_op jit(solution)/shard_map/finish/pallas_call | solution.py:203
  (2 shorter events, 0.0 us)
Async XLA Ops:
  0.6 15.9 %copy-start.7 = (bf16[128,256]{1,0:T(8,128)(2,1)S(1)}, bf16[128,256]{1,0:T(8,128)(2,1)}, u32[]{:S(2)}) copy-start(bf16[128,256]{1,0:T(8,128)(2,1)} %param.12) | copy-start | bytes 196612
  0.6 15.9 %copy-start.6 = (f32[128,256]{1,0:T(8,128)S(1)}, f32[128,256]{1,0:T(8,128)}, u32[]{:S(2)}) copy-start(f32[128,256]{1,0:T(8,128)} %param.11) | copy-start | bytes 393220
  0.7 15.9 %copy-start.5 = (f32[128,256]{1,0:T(8,128)S(1)}, f32[128,256]{1,0:T(8,128)}, u32[]{:S(2)}) copy-start(f32[128,256]{1,0:T(8,128)} %param.10) | copy-start | bytes 393220
  0.7 15.9 %copy-start.4 = (f32[128,256]{1,0:T(8,128)S(1)}, f32[128,256]{1,0:T(8,128)}, u32[]{:S(2)}) copy-start(f32[128,256]{1,0:T(8,128)} %param.9) | copy-start | bytes 393220
  0.7 22.0 %collective-permute-start = (bf16[2,4,1024]{2,1,0:T(4,128)(2,1)}, bf16[2,4,1024]{2,1,0:T(4,128)(2,1)S(1)}, u32[]{:S(2)}, u32[]{:S(2)}) collective-permute-start(bf16[2,4,1024]{2,1,0:T(4,128)(2,1)} %param.13), channel_id=1, source_target_pairs={{0,24},{4,80},{8,152},{12,200},{16,272},{20,344},{24,400},{28,448}... | collective-permute-start | bytes 49160 | tf_op jit(solution)/shard_map/ppermute | solution.py:145
  16.5 32.9 %copy-start.2 = (bf16[2,4,1024]{2,1,0:T(4,128)(2,1)S(1)}, bf16[2,4,1024]{2,1,0:T(4,128)(2,1)}, u32[]{:S(2)}) copy-start(bf16[2,4,1024]{2,1,0:T(4,128)(2,1)} %q_ref) | copy-start | bytes 49156
  16.6 32.8 %copy-start = (bf16[2,2048,128]{2,1,0:T(8,128)(2,1)S(1)}, bf16[2,2048,128]{2,1,0:T(8,128)(2,1)}, u32[]{:S(2)}) copy-start(bf16[2,2048,128]{2,1,0:T(8,128)(2,1)} %k_ref.1) | copy-start | bytes 3145732
  16.6 32.8 %copy-start.1 = (bf16[2,2048,128]{2,1,0:T(8,128)(2,1)S(1)}, bf16[2,2048,128]{2,1,0:T(8,128)(2,1)}, u32[]{:S(2)}) copy-start(bf16[2,2048,128]{2,1,0:T(8,128)(2,1)} %v_ref.1) | copy-start | bytes 3145732
  22.7 13.5 %collective-permute-start.1 = (bf16[512,256]{1,0:T(8,128)(2,1)S(1)}, bf16[512,256]{1,0:T(8,128)(2,1)S(1)}, u32[]{:S(2)}, u32[]{:S(2)}) collective-permute-start(bf16[512,256]{1,0:T(8,128)(2,1)S(1)} %all_gather.3.own_ref), channel_id=1, source_target_pairs={{0,32},{32,0},{1,33},{33,1},{2,34},{34,2},{3,35},{35,3},{4,36},{36... | collective-permute-start | bytes 786440 | tf_op jit(solution)/shard_map/ppermute | solution.py:169
  37.0 12.4 %copy-start.3 = (s32[2]{0:T(128)S(1)}, s32[2]{0:T(128)}, u32[]{:S(2)}) copy-start(s32[2]{0:T(128)} %lengths_ref.1) | copy-start | bytes 28
  37.0 15.8 %all-to-all-start.1 = ((f32[8,8,256]{2,1,0:T(8,128)}), f32[8,8,256]{2,1,0:T(8,128)S(1)}, u32[]{:S(2)}, u32[]{:S(2)}) async-start(f32[8,8,256]{2,1,0:T(8,128)} %project.1), calls=%async_computation.1 | async-start | bytes 131072 | tf_op jit(solution)/shard_map/all_to_all | solution.py:191
